TPU v7x, 32 devices: a whole 2x2x4 slice. The times are simulated.
32 devices in a mesh: dp: 2 (over core), expert: 16 (over z, y, x).
Axes of the slice: x: 2, y: 2, z: 4, core: 2. Of those that a mesh axis runs over, the one named last changes fastest.
Arguments:
- tokens: bfloat16 [6144, 1024], P(('dp', 'expert')), may hold values from -6 to 6
- out_grad: bfloat16 [6144, 1024], P(('dp', 'expert')), may hold values from -2.5 to 2.5
- gates: bfloat16 [6144, 2], P(('dp', 'expert')), may hold values from 0.099609375 to 0.8984375
- expert_ids: int32 [6144, 2], P(('dp', 'expert')), may hold values from 0 to 15, all different within a row; in each aligned block of 192 rows (0 to 191, 192 to 383, ...) at most 36 rows name the same one
- w_in: bfloat16 [16, 1024, 1024], P('expert', None, 'dp'), may hold values from -0.1875 to 0.1875
- w_out: bfloat16 [16, 1024, 1024], P('expert', None, 'dp'), may hold values from -0.1875 to 0.1875
Outputs:
- d_tokens: bfloat16 [6144, 1024], P(('dp', 'expert'))
- gate_grad: bfloat16 [6144, 2], P(('dp', 'expert'))
- grad_in: float32 [16, 1024, 1024], P('expert', None, 'dp')
- grad_out: float32 [16, 1024, 1024], P('expert', None, 'dp')
Inputs may be any that keep to these rules, and one draw needn't show every extreme that they name: `expert_ids`: each row names two different experts. Among the 192 rows of one device no expert is named more than 36 times, and in every draw some device names some expert exactly 36 times.
All inputs are finite; a program needn't handle non-finite values.
Results may differ from a plain program's by a relative error of at most 0.022.
Values may be sent and summed in bfloat16 or wider, within the bound.
A program may use at most 64 MiB of HBM per device.

v0:
```python
import jax
import jax.numpy as jnp
from jax import lax
from jax.sharding import PartitionSpec as P

gelu_scale = 0.7978845608028654
cubic_coef = 0.044715


def gelu_value(values):
    return (
        0.5
        * values
        * (1.0 + jnp.tanh(gelu_scale * (values + cubic_coef * values * values * values)))
    )


def gelu_slope(values):
    tanh_inner = jnp.tanh(gelu_scale * (values + cubic_coef * values * values * values))
    return 0.5 * (1.0 + tanh_inner) + 0.5 * values * (
        1.0 - tanh_inner * tanh_inner
    ) * gelu_scale * (1.0 + 3.0 * cubic_coef * values * values)


def slot_positions(expert_ids, experts, capacity):
    flat_ids = expert_ids.reshape(-1)
    onehot = (flat_ids[:, None] == jnp.arange(experts, dtype=jnp.int32)[None, :]).astype(jnp.int32)
    earlier = jnp.cumsum(onehot, axis=0) - onehot
    return flat_ids * capacity + jnp.sum(earlier * onehot, axis=1)


def column_terms(rows_x, rows_dy, gate_column, w_first, w_second):
    pre_act = jnp.dot(rows_x, w_first, preferred_element_type=jnp.float32)
    activated = gelu_value(pre_act).astype(jnp.bfloat16)
    dy_proj = jnp.dot(rows_dy, w_second, preferred_element_type=jnp.float32)
    d_pre = (gate_column * dy_proj * gelu_slope(pre_act)).astype(jnp.bfloat16)
    scaled = (gate_column * activated.astype(jnp.float32)).astype(jnp.bfloat16)
    dx_part = lax.dot_general(
        d_pre, w_first, (((1,), (1,)), ((), ())), preferred_element_type=jnp.float32
    )
    gate_part = lax.dot_general(
        activated, w_second, (((1,), (1,)), ((), ())), preferred_element_type=jnp.float32
    )
    return (dx_part, gate_part, d_pre, scaled)


def gate_value(gate_part, rows_dy):
    result = jnp.sum(rows_dy.astype(jnp.float32) * gate_part, axis=1)
    return result


def shards(tokens, out_grad, gates, expert_ids, w_in, w_out):
    tok_rows = tokens.shape[0]
    model_width = tokens.shape[1]
    experts = lax.axis_size("expert")
    capacity = 3 * tok_rows // experts
    slot_count = experts * capacity
    target = slot_positions(expert_ids, experts, capacity)
    source_row = (
        jnp.zeros((slot_count,), jnp.int32)
        .at[target]
        .set(jnp.arange(2 * tok_rows, dtype=jnp.int32) // 2)
    )
    filled = jnp.zeros((slot_count,), jnp.bool_).at[target].set(True)
    send_x = jnp.where(filled[:, None], tokens[source_row], jnp.zeros((), jnp.bfloat16)).reshape(
        experts, capacity, model_width
    )
    send_dy = jnp.where(filled[:, None], out_grad[source_row], jnp.zeros((), jnp.bfloat16)).reshape(
        experts, capacity, model_width
    )
    send_gate = (
        jnp.zeros((slot_count,), jnp.bfloat16)
        .at[target]
        .set(gates.reshape(-1))
        .reshape(experts, capacity)
    )
    got_x, got_dy, got_gate = (
        lax.all_to_all(send_x, "expert", split_axis=0, concat_axis=0, tiled=True),
        lax.all_to_all(send_dy, "expert", split_axis=0, concat_axis=0, tiled=True),
        lax.all_to_all(send_gate, "expert", split_axis=0, concat_axis=0, tiled=True),
    )
    rows_x = got_x.reshape(slot_count, model_width)
    rows_dy = got_dy.reshape(slot_count, model_width)
    gate_column = got_gate.reshape(slot_count, 1).astype(jnp.float32)
    full_in, full_out = (
        lax.all_gather(w_in, "dp", axis=2, tiled=True),
        lax.all_gather(w_out, "dp", axis=2, tiled=True),
    )
    dx_part, gate_part, d_pre, scaled = column_terms(
        rows_x, rows_dy, gate_column, full_in[0], full_out[0]
    )
    dx_rows = dx_part.astype(jnp.bfloat16).reshape(experts, capacity, model_width)
    gate_rows = gate_value(gate_part, rows_dy).astype(jnp.bfloat16).reshape(experts, capacity)
    back_dx, back_gate = (
        lax.all_to_all(dx_rows, "expert", split_axis=0, concat_axis=0, tiled=True),
        lax.all_to_all(gate_rows, "expert", split_axis=0, concat_axis=0, tiled=True),
    )
    grad_first = lax.dot_general(
        rows_x, d_pre, (((0,), (0,)), ((), ())), preferred_element_type=jnp.float32
    )
    grad_second = lax.dot_general(
        rows_dy, scaled, (((0,), (0,)), ((), ())), preferred_element_type=jnp.float32
    )
    grad_in, grad_out = (
        lax.psum_scatter(
            grad_first[None].astype(jnp.bfloat16), "dp", scatter_dimension=2, tiled=True
        ).astype(jnp.float32),
        lax.psum_scatter(
            grad_second[None].astype(jnp.bfloat16), "dp", scatter_dimension=2, tiled=True
        ).astype(jnp.float32),
    )
    picked = back_dx.reshape(slot_count, model_width)[target].reshape(tok_rows, 2, model_width)
    d_tokens = jnp.sum(picked.astype(jnp.float32), axis=1).astype(jnp.bfloat16)
    gate_grad = back_gate.reshape(slot_count)[target].reshape(tok_rows, 2)
    return (d_tokens, gate_grad, grad_in, grad_out)


def solution(mesh):
    in_specs = (
        P(("dp", "expert"), None),
        P(("dp", "expert"), None),
        P(("dp", "expert"), None),
        P(("dp", "expert"), None),
        P("expert", None, "dp"),
        P("expert", None, "dp"),
    )
    out_specs = (
        P(("dp", "expert"), None),
        P(("dp", "expert"), None),
        P("expert", None, "dp"),
        P("expert", None, "dp"),
    )
    return jax.shard_map(shards, mesh=mesh, in_specs=in_specs, out_specs=out_specs, check_vma=False)
```

profile of v0, /device:TPU:0, one launch (start us, length us, event | category | flops | bytes accessed | tf_op | source)
XLA Modules:
  0.0 199.1 jit_solution(995444362738109422)
XLA Ops:
  7.2 0.0 copy-start
  7.2 0.7 broadcast_multiply_fusion
  7.9 0.8 copy.17
  8.7 0.1 eq.29
  8.9 0.1 eq.25
  9.0 0.8 copy.20
  9.8 0.2 reshape.171
  10.0 0.1 copy.16
  10.1 0.1 mul.88
  10.3 0.9 reduce-window.6
  11.1 0.2 slice_reduce_fusion
  11.4 0.1 fusion.25
  11.5 3.0 %scatter_custom_fusion = bf16[576]{0:T(1024)(128)(2,1)S(1)} fusion(s32[384]{0:T(512)S(1)} %fusion.34, bf16[384]{0:T(512)(128)(2,1)S(1)} %reshape.171, bf16[]{:T(256)} %constant.15.clone.1), kind=kCustom, calls=%fused_computation.60 | custom fusion | bytes 1154 | tf_op jit(solution)/shard_map/scatter | solution.py:74
  14.5 0.7 all_to_all.25
  15.2 8.3 %all-to-all-start = ((bf16[16,1,36]{2,1,0:T(2,128)(2,1)}), bf16[16,1,36]{2,1,0:T(2,128)(2,1)S(1)}, u32[]{:S(2)}, u32[]{:S(2)}) async-start(bf16[16,1,36]{2,1,0:T(2,128)(2,1)} %all_to_all.25), calls=%async_computation | async-start | bytes 16384 | tf_op jit(solution)/shard_map/all_to_all | solution.py:80
  23.5 2.0 scatter_custom_fusion.1
  25.5 0.1 broadcast_in_dim.44
  25.6 2.9 %scatter_custom_fusion.2 = s32[576]{0:T(1024)S(1)} fusion(s32[384]{0:T(512)S(1)} %fusion.34, s32[384]{0:T(512)S(1)} %add_select_fusion, s32[]{:T(128)} %constant.17.clone.1), kind=kCustom, calls=%fused_computation.53 | custom fusion | bytes 2308 | tf_op jit(solution)/shard_map/scatter | solution.py:62
  28.6 2.9 %gather_fusion.1 = bf16[576,1024]{1,0:T(8,128)(2,1)S(1)} fusion(bf16[192,1024]{1,0:T(8,128)(2,1)S(1)} %copy-done, s32[1024]{0:T(1024)S(1)} %pad_clamp_fusion.1), kind=kCustom, calls=%fused_computation.1 | custom fusion | bytes 2361600 | tf_op jit(solution)/shard_map/gather | solution.py:65
  31.4 0.3 gather.19
  31.7 0.7 copy-done.1
  32.4 3.4 %gather_fusion = bf16[576,1024]{1,0:T(8,128)(2,1)} fusion(bf16[192,1024]{1,0:T(8,128)(2,1)S(1)} %copy-done.1, s32[1024]{0:T(1024)S(1)} %pad_clamp_fusion.1), kind=kCustom, calls=%fused_computation | custom fusion | bytes 2361600 | tf_op jit(solution)/shard_map/gather | solution.py:68
  35.8 1.4 gather.17
  37.2 1.7 broadcast_select_fusion.1
  39.0 6.9 %all-to-all-start.1 = ((bf16[16,36,1024]{2,1,0:T(8,128)(2,1)}), bf16[16,36,1024]{2,1,0:T(8,128)(2,1)S(1)}, u32[]{:S(2)}, u32[]{:S(2)}) async-start(bf16[16,36,1024]{2,1,0:T(8,128)(2,1)} %get-tuple-element.12), calls=%async_computation.1 | async-start | bytes 2621440 | tf_op jit(solution)/shard_map/all_to_all | solution.py:79
  45.9 0.0 all-gather.5.cloned.1.call-start
  45.9 0.7 all-gather.5.cloned.1.call-update
  46.6 28.3 %all-to-all-done.1 = bf16[16,36,1024]{2,1,0:T(8,128)(2,1)S(1)} async-done(((bf16[16,36,1024]{2,1,0:T(8,128)(2,1)}), bf16[16,36,1024]{2,1,0:T(8,128)(2,1)S(1)}, u32[]{:S(2)}, u32[]{:S(2)}) %all-to-all-start.1) | async-done | bytes 1179680 | tf_op jit(solution)/shard_map/all_to_all | solution.py:79
  74.9 6.3 %all-to-all-start.2 = ((bf16[16,36,1024]{2,1,0:T(8,128)(2,1)}), bf16[16,36,1024]{2,1,0:T(8,128)(2,1)S(1)}, u32[]{:S(2)}, u32[]{:S(2)}) async-start(bf16[16,36,1024]{2,1,0:T(8,128)(2,1)} %get-tuple-element.13), calls=%async_computation.2 | async-start | bytes 2621440 | tf_op jit(solution)/shard_map/all_to_all | solution.py:78
  81.2 0.0 all-gather.3.cloned.1.call-start
  81.3 0.7 all-gather.3.cloned.1.call-update
  82.0 0.2 reduce-scatter.5.cloned.1.call-start
  82.2 0.1 reshape.134
  82.3 1.1 reshape.127
  83.4 26.3 %all-to-all-done.2 = bf16[16,36,1024]{2,1,0:T(8,128)(2,1)S(1)} async-done(((bf16[16,36,1024]{2,1,0:T(8,128)(2,1)}), bf16[16,36,1024]{2,1,0:T(8,128)(2,1)S(1)}, u32[]{:S(2)}, u32[]{:S(2)}) %all-to-all-start.2) | async-done | bytes 1179680 | tf_op jit(solution)/shard_map/all_to_all | solution.py:78
  109.8 1.1 reshape.128
  110.9 3.4 %fusion.9 = f32[576,1024]{1,0:T(8,128)S(1)} fusion(bf16[576,1024]{1,0:T(8,128)(2,1)} %reshape.128, bf16[1,1024,1024]{2,1,0:T(8,128)(2,1)} %all-gather.5.cloned.1.call-done), kind=kOutput, calls=%fused_computation.21 | convolution fusion | flops 1207959552 | bytes 5636096 | tf_op jit(solution)/shard_map/dot_general | solution.py:33
  114.3 1.4 copy-done.4
  115.7 3.6 %convert_bitcast_fusion = bf16[1,1024,1024]{2,1,0:T(8,128)(2,1)} fusion(bf16[576,1024]{1,0:T(8,128)(2,1)S(1)} %copy-done.2, f32[576]{0:T(1024)S(1)} %reshape.134, f32[576,1024]{1,0:T(8,128)S(1)} %fusion.9), kind=kOutput, calls=%fused_computation.27 | convolution fusion | flops 1216086016 | bytes 5638400 | tf_op jit(solution)/shard_map/dot_general | solution.py:101
  119.3 0.0 reduce-scatter.5.cloned.1.call-update
  119.4 0.0 reduce-scatter.3.cloned.1.call-start
  119.4 0.0 all-gather.3.cloned.1.call-done
  119.5 4.8 %fusion.6 = bf16[576,1024]{1,0:T(8,128)(2,1)S(1)} fusion(f32[576,1024]{1,0:T(8,128)} %copy-done.4, bf16[576,1024]{1,0:T(8,128)(2,1)S(1)} %copy-done.2, bf16[1,1024,1024]{2,1,0:T(8,128)(2,1)} %all-gather.3.cloned.1.call-done, f32[576]{0:T(1024)S(1)} %reshape.134), kind=kOutput, calls=%fused_computation.15 | convolution fusion | flops 1219756032 | bytes 6818048 | tf_op jit(solution)/shard_map/dot_general | solution.py:35
  124.2 1.0 copy-done.5
  125.2 3.2 %convert_bitcast_fusion.1 = bf16[1,1024,1024]{2,1,0:T(8,128)(2,1)} fusion(bf16[576,1024]{1,0:T(8,128)(2,1)S(1)} %copy-done.3, bf16[576,1024]{1,0:T(8,128)(2,1)S(1)} %fusion.6), kind=kOutput, calls=%fused_computation.28 | convolution fusion | flops 1209008128 | bytes 4456448 | tf_op jit(solution)/shard_map/dot_general | solution.py:98
  128.4 0.0 reduce-scatter.3.cloned.1.call-update
  128.4 4.3 %multiply_reduce_fusion = bf16[576]{0:T(1024)(128)(2,1)S(1)} fusion(bf16[576,1024]{1,0:T(8,128)(2,1)S(1)} %copy-done.2, bf16[1,1024,1024]{2,1,0:T(8,128)(2,1)} %all-gather.3.cloned.1.call-done, f32[576,1024]{1,0:T(8,128)} %copy-done.4), kind=kOutput, calls=%fused_computation.17 | convolution fusion | flops 1215036928 | bytes 5637248 | tf_op jit(solution)/shard_map/dot_general | solution.py:41
  132.7 0.7 convert_element_type.89
  133.4 6.4 %all-to-all-start.4 = ((bf16[16,1,36]{2,1,0:T(2,128)(2,1)}), bf16[16,1,36]{2,1,0:T(2,128)(2,1)S(1)}, u32[]{:S(2)}, u32[]{:S(2)}) async-start(bf16[16,1,36]{2,1,0:T(2,128)(2,1)} %convert_element_type.89), calls=%async_computation.4 | async-start | bytes 16384 | tf_op jit(solution)/shard_map/all_to_all | solution.py:96
  139.9 3.1 %fusion.17 = bf16[576,1024]{1,0:T(8,128)(2,1)S(1)} fusion(bf16[576,1024]{1,0:T(8,128)(2,1)S(1)} %copy-done.6, bf16[1,1024,1024]{2,1,0:T(8,128)(2,1)} %all-gather.5.cloned.1.call-done), kind=kOutput, calls=%fused_computation.29 | convolution fusion | flops 1208549376 | bytes 4456448 | tf_op jit(solution)/shard_map/dot_general | solution.py:38
  143.0 1.2 reshape.129
  144.2 2.9 %all-to-all-done.4 = bf16[16,1,36]{2,1,0:T(2,128)(2,1)S(1)} async-done(((bf16[16,1,36]{2,1,0:T(2,128)(2,1)}), bf16[16,1,36]{2,1,0:T(2,128)(2,1)S(1)}, u32[]{:S(2)}, u32[]{:S(2)}) %all-to-all-start.4) | async-done | bytes 1184 | tf_op jit(solution)/shard_map/all_to_all | solution.py:96
  147.1 4.0 %all-to-all-start.3 = ((bf16[16,36,1024]{2,1,0:T(8,128)(2,1)}), bf16[16,36,1024]{2,1,0:T(8,128)(2,1)S(1)}, u32[]{:S(2)}, u32[]{:S(2)}) async-start(bf16[16,36,1024]{2,1,0:T(8,128)(2,1)} %reshape.129), calls=%async_computation.3 | async-start | bytes 2621440 | tf_op jit(solution)/shard_map/all_to_all | solution.py:95
  151.1 0.1 reshape.132
  151.2 2.8 %gather_fusion.3 = bf16[384]{0:T(512)(128)(2,1)S(1)} fusion(bf16[576]{0:T(1024)(128)(2,1)S(1)} %reshape.132, s32[1024]{0:T(1024)S(1)} %pad_clamp_fusion), kind=kCustom, calls=%fused_computation.3 | custom fusion | bytes 3072 | tf_op jit(solution)/shard_map/gather | solution.py:114
  154.0 0.2 reshape.133
  154.2 0.7 copy.23
  154.9 24.1 %all-to-all-done.3 = bf16[16,36,1024]{2,1,0:T(8,128)(2,1)S(1)} async-done(((bf16[16,36,1024]{2,1,0:T(8,128)(2,1)}), bf16[16,36,1024]{2,1,0:T(8,128)(2,1)S(1)}, u32[]{:S(2)}, u32[]{:S(2)}) %all-to-all-start.3) | async-done | bytes 1179680 | tf_op jit(solution)/shard_map/all_to_all | solution.py:95
  179.0 0.3 reshape.130
  179.2 2.7 %gather_fusion.2 = bf16[384,1024]{1,0:T(8,128)(2,1)} fusion(bf16[576,1024]{1,0:T(8,128)(2,1)S(1)} %reshape.130, s32[1024]{0:T(1024)S(1)} %pad_clamp_fusion), kind=kCustom, calls=%fused_computation.2 | custom fusion | bytes 1574400 | tf_op jit(solution)/shard_map/gather | solution.py:112
  181.9 2.1 %reshape.131 = bf16[192,2,1024]{2,1,0:T(2,128)(2,1)S(1)} reshape(bf16[384,1024]{1,0:T(8,128)(2,1)} %gather_fusion.2) | data formatting | bytes 1572864 | tf_op jit(solution)/shard_map/reshape | solution.py:112
  184.1 2.8 %reduce_sum.34 = bf16[192,1024]{1,0:T(8,128)(2,1)} reduce(bf16[192,2,1024]{2,1,0:T(2,128)(2,1)S(1)} %reshape.131, bf16[]{:T(256)} %constant.15.clone.1), dimensions={1}, to_apply=%region_6.7 | reduce | flops 196608 | bytes 1179650 | tf_op jit(solution)/shard_map/reduce_sum | solution.py:113
  186.9 2.8 %convert_element_type.87 = f32[1,1024,512]{2,1,0:T(8,128)} convert(bf16[1,1024,512]{2,1,0:T(8,128)(2,1)} %reduce-scatter.5.cloned.1.call-done) | non-fusion elementwise | flops 524288 | bytes 3145728 | tf_op jit(solution)/shard_map/convert_element_type | solution.py:110
  189.7 2.8 %convert_element_type.82 = f32[1,1024,512]{2,1,0:T(8,128)} convert(bf16[1,1024,512]{2,1,0:T(8,128)(2,1)} %reduce-scatter.3.cloned.1.call-done) | non-fusion elementwise | flops 524288 | bytes 3145728 | tf_op jit(solution)/shard_map/convert_element_type | solution.py:107
  (24 shorter events, 0.2 us)
Async XLA Ops:
  7.2 21.4 %copy-start = (bf16[192,1024]{1,0:T(8,128)(2,1)S(1)}, bf16[192,1024]{1,0:T(8,128)(2,1)}, u32[]{:S(2)}) copy-start(bf16[192,1024]{1,0:T(8,128)(2,1)} %param.6) | copy-start | bytes 1179652
  15.2 23.8 %all-to-all-start = ((bf16[16,1,36]{2,1,0:T(2,128)(2,1)}), bf16[16,1,36]{2,1,0:T(2,128)(2,1)S(1)}, u32[]{:S(2)}, u32[]{:S(2)}) async-start(bf16[16,1,36]{2,1,0:T(2,128)(2,1)} %all_to_all.25), calls=%async_computation | async-start | bytes 16384 | tf_op jit(solution)/shard_map/all_to_all | solution.py:80
  31.4 1.0 copy-start.1
  39.0 35.9 %all-to-all-start.1 = ((bf16[16,36,1024]{2,1,0:T(8,128)(2,1)}), bf16[16,36,1024]{2,1,0:T(8,128)(2,1)S(1)}, u32[]{:S(2)}, u32[]{:S(2)}) async-start(bf16[16,36,1024]{2,1,0:T(8,128)(2,1)} %get-tuple-element.12), calls=%async_computation.1 | async-start | bytes 2621440 | tf_op jit(solution)/shard_map/all_to_all | solution.py:79
  45.9 65.0 %all-gather.5.cloned.1.call-start = ((), (), s32[]{:S(2)}) async-start(), calls=%async_computation.8 | async-start | bytes 3145728 | tf_op jit(solution)/shard_map/all_gather | solution.py:86
  74.9 34.9 %all-to-all-start.2 = ((bf16[16,36,1024]{2,1,0:T(8,128)(2,1)}), bf16[16,36,1024]{2,1,0:T(8,128)(2,1)S(1)}, u32[]{:S(2)}, u32[]{:S(2)}) async-start(bf16[16,36,1024]{2,1,0:T(8,128)(2,1)} %get-tuple-element.13), calls=%async_computation.2 | async-start | bytes 2621440 | tf_op jit(solution)/shard_map/all_to_all | solution.py:78
  81.2 38.2 %all-gather.3.cloned.1.call-start = ((), (), s32[]{:S(2)}) async-start(), calls=%async_computation.7 | async-start | bytes 3145728 | tf_op jit(solution)/shard_map/all_gather | solution.py:87
  82.0 104.9 %reduce-scatter.5.cloned.1.call-start = ((), (), s32[]{:S(2)}) async-start(), calls=%async_computation.10 | async-start | bytes 3145728 | tf_op jit(solution)/shard_map/reduce_scatter | solution.py:108
  110.9 4.8 %copy-start.2 = (bf16[576,1024]{1,0:T(8,128)(2,1)S(1)}, bf16[576,1024]{1,0:T(8,128)(2,1)}, u32[]{:S(2)}) copy-start(bf16[576,1024]{1,0:T(8,128)(2,1)} %reshape.127) | copy-start | bytes 3538948
  114.3 1.4 copy-start.4
  119.4 5.9 %copy-start.3 = (bf16[576,1024]{1,0:T(8,128)(2,1)S(1)}, bf16[576,1024]{1,0:T(8,128)(2,1)}, u32[]{:S(2)}) copy-start(bf16[576,1024]{1,0:T(8,128)(2,1)} %reshape.128) | copy-start | bytes 3538948
  119.4 70.4 %reduce-scatter.3.cloned.1.call-start = ((), (), s32[]{:S(2)}) async-start(), calls=%async_computation.9 | async-start | bytes 3145728 | tf_op jit(solution)/shard_map/reduce_scatter | solution.py:105
  124.2 1.0 copy-start.5
  128.4 11.4 %copy-start.6 = (bf16[576,1024]{1,0:T(8,128)(2,1)S(1)}, bf16[576,1024]{1,0:T(8,128)(2,1)}, u32[]{:S(2)}) copy-start(bf16[576,1024]{1,0:T(8,128)(2,1)} %copy-done.5) | copy-start | bytes 3538948
  133.4 13.6 %all-to-all-start.4 = ((bf16[16,1,36]{2,1,0:T(2,128)(2,1)}), bf16[16,1,36]{2,1,0:T(2,128)(2,1)S(1)}, u32[]{:S(2)}, u32[]{:S(2)}) async-start(bf16[16,1,36]{2,1,0:T(2,128)(2,1)} %convert_element_type.89), calls=%async_computation.4 | async-start | bytes 16384 | tf_op jit(solution)/shard_map/all_to_all | solution.py:96
  147.1 31.9 %all-to-all-start.3 = ((bf16[16,36,1024]{2,1,0:T(8,128)(2,1)}), bf16[16,36,1024]{2,1,0:T(8,128)(2,1)S(1)}, u32[]{:S(2)}, u32[]{:S(2)}) async-start(bf16[16,36,1024]{2,1,0:T(8,128)(2,1)} %reshape.129), calls=%async_computation.3 | async-start | bytes 2621440 | tf_op jit(solution)/shard_map/all_to_all | solution.py:95
Sparse Core Ops, SparseCore 0:
  48.3 11.8 all-gather.4
  83.6 11.8 all-gather.2
  119.5 10.3 reduce-scatter.4
  132.6 10.8 reduce-scatter.2
where the time goes:
time: 201 us; the launch traced here: 199 us
  waiting for transfers between devices  83 us (41%)
  local copies, waits for them, and re-layouts  35.3 us (18%)
  starting transfers between devices  32.3 us (16%)
  matrix products  22.3 us (11%)
  between operations  14.1 us (7%)
  other arithmetic  12.1 us (6%)
    all_to_all x1, waiting for transfers between devices, shards(): lax.all_to_all(send_dy, 'expert', split_axis=0, concat_axis=0, tiled=True)  28.3 us
    all_to_all x1, waiting for transfers between devices, shards(): lax.all_to_all(send_x, 'expert', split_axis=0, concat_axis=0, tiled=True)  26.3 us
    all_to_all x1, waiting for transfers between devices, shards(): lax.all_to_all(dx_rows, 'expert', split_axis=0, concat_axis=0, tiled=True)  24.1 us
    all_to_all x1, starting transfers between devices, shards(): lax.all_to_all(send_gate, 'expert', split_axis=0, concat_axis=0, tiled=True)  8.31 us
    all_to_all x1, starting transfers between devices, shards(): lax.all_to_all(send_dy, 'expert', split_axis=0, concat_axis=0, tiled=True)  6.91 us
    all_to_all x1, starting transfers between devices, shards(): lax.all_to_all(gate_rows, 'expert', split_axis=0, concat_axis=0, tiled=True)  6.44 us
    all_to_all x1, starting transfers between devices, shards(): lax.all_to_all(send_x, 'expert', split_axis=0, concat_axis=0, tiled=True)  6.32 us
    convert_element_type x2, other arithmetic, shards(): grad_in, grad_out = (lax.psum_scatter(grad_first[None].astype(jnp.bfloat1...  5.67 us
  transfers between devices with their start and end apart: 9, of which 4 were waited for; matrix products, arithmetic and copies ran while one was open for 28% of the time, Pallas kernels for 0%

commit v1 on v0

v1 whole, which is shorter than its diff:
```python
import functools

import jax
import jax.numpy as jnp
from jax import lax
from jax.experimental import pallas as pl
from jax.experimental.pallas import tpu as pltpu
from jax.sharding import PartitionSpec as P

gelu_scale = 0.7978845608028654
cubic_coef = 0.044715
MESH = pl.DeviceIdType.MESH
GROUPS = 4
BF = jnp.bfloat16
F32 = jnp.float32


def paired(group, step):
    return 2 * ((group // 2 + step // 2) % 2) + (group % 2 + step % 2) % 2


def contract_first(a, b):
    return lax.dot_general(a, b, (((0,), (0,)), ((), ())), preferred_element_type=F32)


def contract_last(a, b):
    return lax.dot_general(a, b, (((1,), (1,)), ((), ())), preferred_element_type=F32)


def matmul(a, b):
    return jnp.dot(a, b, preferred_element_type=F32)


def lanes(rows, columns):
    return lax.broadcasted_iota(jnp.int32, (rows, columns), 1)


def ones_at(*conditions):
    hit = conditions[0]
    for other in conditions[1:]:
        hit = hit | other
    return jnp.where(hit, 1.0, 0.0).astype(BF)


def kernel(
    experts,
    parts,
    cap,
    chunk,
    tokens_ref,
    out_grad_ref,
    gates_ref,
    ids_ref,
    w_in_ref,
    w_out_ref,
    d_tokens_ref,
    gate_grad_ref,
    sums_in_ref,
    sums_out_ref,
    send_buf,
    recv_buf,
    ret_buf,
    back_buf,
    pick_x,
    pick_dy,
    pick_gate,
    weights_in,
    weights_out,
    rows_x,
    rows_dy,
    d_pre,
    scaled,
    part_in,
    part_out,
    send_sem,
    recv_sem,
    ret_sem,
    back_sem,
    w_send_sem,
    w_recv_sem,
    g_send_sem,
    g_recv_sem,
):
    size = experts // GROUPS
    span = size * chunk
    slots = size * cap
    tok_rows, width = tokens_ref.shape
    half = width // 2
    hidden = w_in_ref.shape[2]
    me = lax.axis_index("expert")
    my_dp = lax.axis_index("dp")
    my_group, my_member = me // size, me % size

    def expert_device(group, member):
        return {"expert": group * size + member}

    barrier = pltpu.get_barrier_semaphore()
    for step in range(GROUPS):
        for turn in range(size):
            if step or turn:
                pl.semaphore_signal(
                    barrier,
                    inc=1,
                    device_id=expert_device(paired(my_group, step), (my_member + turn) % size),
                    device_id_type=MESH,
                )
    for turn in range(1, parts):
        pl.semaphore_signal(
            barrier, inc=1, device_id={"dp": (my_dp + turn) % parts}, device_id_type=MESH
        )

    own_w = [
        pltpu.make_async_copy(w_in_ref.at[0], weights_in.at[0], w_recv_sem.at[0, 0]),
        pltpu.make_async_copy(w_out_ref.at[0], weights_out.at[0], w_recv_sem.at[1, 0]),
    ]
    for copy in own_w:
        copy.start()

    ids = ids_ref[...]
    id_0, id_1 = ids[:, 0:1], ids[:, 1:2]
    named = lanes(tok_rows, 128)
    named_0, named_1 = named == id_0, named == id_1
    later = lax.broadcasted_iota(jnp.int32, (tok_rows, tok_rows), 0) > lanes(tok_rows, tok_rows)
    earlier = matmul(ones_at(later), ones_at(named_0, named_1))
    slot_0 = jnp.sum(jnp.where(named_0, earlier, 0.0), axis=1, keepdims=True).astype(jnp.int32)
    slot_1 = jnp.sum(jnp.where(named_1, earlier, 0.0), axis=1, keepdims=True).astype(jnp.int32)
    place_0, place_1 = id_0 * chunk + slot_0, id_1 * chunk + slot_1
    line_0, line_1 = id_0 * chunk + 2 * cap, id_1 * chunk + 2 * cap
    at_slot_0, at_slot_1 = named == slot_0, named == slot_1
    gates = gates_ref[...].astype(F32)
    gate_0 = jnp.where(at_slot_0, gates[:, 0:1], 0.0).astype(BF)
    gate_1 = jnp.where(at_slot_1, gates[:, 1:2], 0.0).astype(BF)

    def selectors(group):
        lane = lanes(tok_rows, span) + group * span
        return (
            ones_at(lane == place_0, lane == place_1),
            ones_at(lane == place_0 + cap, lane == place_1 + cap),
            ones_at(lane == line_0),
            ones_at(lane == line_1),
        )

    def chunk_rows(member):
        return pl.ds(pl.multiple_of(member * chunk, 16), chunk)

    def dispatch_copy(group, member):
        return pltpu.make_async_remote_copy(
            src_ref=send_buf.at[group, chunk_rows(member)],
            dst_ref=recv_buf.at[my_group, chunk_rows(my_member)],
            send_sem=send_sem.at[group * size + member],
            recv_sem=recv_sem.at[me],
            device_id=expert_device(group, member),
            device_id_type=MESH,
        )

    def return_copy(group, member):
        return pltpu.make_async_remote_copy(
            src_ref=ret_buf.at[group, chunk_rows(member)],
            dst_ref=back_buf.at[my_group, chunk_rows(my_member)],
            send_sem=ret_sem.at[group * size + member],
            recv_sem=back_sem.at[me],
            device_id=expert_device(group, member),
            device_id_type=MESH,
        )

    def local_copy(source, target, sems):
        return pltpu.make_async_copy(
            source.at[my_group, chunk_rows(my_member)],
            target.at[my_group, chunk_rows(my_member)],
            sems.at[me],
        )

    def await_group(target, sems, group):
        for member in range(size):
            block = target.at[group, pl.ds(member * chunk, chunk)]
            pltpu.make_async_copy(block, block, sems.at[group * size + member]).wait()

    def fill(group):
        to_x, to_dy, to_line_0, to_line_1 = selectors(group)
        packed = contract_first(to_x, tokens_ref[...]) + contract_first(to_dy, out_grad_ref[...])
        line = contract_first(to_line_0, gate_0) + contract_first(to_line_1, gate_1)
        send_buf[group, :, 128:] = packed[:, 128:].astype(BF)
        send_buf[group, :, :128] = (packed[:, :128] + line).astype(BF)

    for step in (3, 2, 1, 0):
        group = paired(my_group, step)
        fill(group)
        if step == 3:
            pl.semaphore_wait(barrier, experts - 1 + parts - 1)
        for turn in range(size):
            member = (my_member + turn) % size
            if step or turn:
                dispatch_copy(group, member).start()
            else:
                local_copy(send_buf, recv_buf, recv_sem).start()
        if step == 3:
            for turn in range(1, parts):
                for n, (source, target) in enumerate(
                    ((w_in_ref, weights_in), (w_out_ref, weights_out))
                ):
                    pltpu.make_async_remote_copy(
                        src_ref=source.at[0],
                        dst_ref=target.at[parts - turn],
                        send_sem=w_send_sem.at[n, turn],
                        recv_sem=w_recv_sem.at[n, parts - turn],
                        device_id={"dp": (my_dp + turn) % parts},
                        device_id_type=MESH,
                    ).start()

    slot = lax.broadcasted_iota(jnp.int32, (slots, 1), 0)
    first = (slot // cap) * chunk
    within = slot % cap
    pick_x[...] = ones_at(lanes(slots, span) == first + within)
    pick_dy[...] = ones_at(lanes(slots, span) == first + within + cap)
    pick_gate[...] = ones_at(lanes(slots, span) == first + 2 * cap)
    at_within = lanes(slots, 128) == within

    for copy in own_w:
        copy.wait()
    for part in range(1, parts):
        for n, target in enumerate((weights_in, weights_out)):
            block = target.at[part]
            pltpu.make_async_copy(block, block, w_recv_sem.at[n, part]).wait()

    order = (0, 1, 3, 2)

    def work(turn_index, carry):
        step = turn_index + (turn_index // 2) * (5 - 2 * turn_index)
        group = paired(my_group, step)
        await_group(recv_buf, recv_sem, group)
        rows = pl.ds(pl.multiple_of(turn_index * slots, 16), slots)
        got = recv_buf[group]
        x = matmul(pick_x[...], got).astype(BF)
        dy = matmul(pick_dy[...], got).astype(BF)
        lines = matmul(pick_gate[...], got[:, :128])
        gate = jnp.sum(jnp.where(at_within, lines, 0.0), axis=1, keepdims=True)
        rows_x[rows] = x
        rows_dy[rows] = dy
        dx = None
        gate_slot = None
        for part in range(parts):
            v = matmul(x, weights_in[part])
            dy_proj = matmul(dy, weights_out[part])
            tanh_inner = jnp.tanh(gelu_scale * (v + cubic_coef * v * v * v))
            activated = (0.5 * v * (1.0 + tanh_inner)).astype(BF).astype(F32)
            slope = 0.5 * (1.0 + tanh_inner) + 0.5 * v * (
                1.0 - tanh_inner * tanh_inner
            ) * gelu_scale * (1.0 + 3.0 * cubic_coef * v * v)
            d_pre_part = (gate * dy_proj * slope).astype(BF)
            d_pre[part, rows] = d_pre_part
            scaled[part, rows] = (gate * activated).astype(BF)
            gate_part = jnp.sum(activated * dy_proj, axis=1, keepdims=True)
            dx_part = contract_last(d_pre_part, weights_in[part])
            dx = dx_part if dx is None else dx + dx_part
            gate_slot = gate_part if gate_slot is None else gate_slot + gate_part
        dx = dx.astype(BF)
        packed = contract_first(pick_x[...], dx[:, :half]) + contract_first(
            pick_dy[...], dx[:, half:]
        )
        line = contract_first(pick_gate[...], jnp.where(at_within, gate_slot, 0.0).astype(BF))
        ret_buf[group, :, 128:] = packed[:, 128:].astype(BF)
        ret_buf[group, :, :128] = (packed[:, :128] + line).astype(BF)

        for turn in range(1, size):
            return_copy(group, (my_member + turn) % size).start()

        @pl.when(turn_index == 0)
        def _():
            local_copy(ret_buf, back_buf, back_sem).start()

        @pl.when(turn_index > 0)
        def _():
            return_copy(group, my_member).start()

        return carry

    lax.fori_loop(0, GROUPS, work, 0)

    tile = 256

    def grad_copy(n, part):
        source, target = ((part_in, sums_in_ref), (part_out, sums_out_ref))[n]
        if part == 0:
            return pltpu.make_async_copy(source.at[0], target.at[0], g_recv_sem.at[n, 0])
        return pltpu.make_async_remote_copy(
            src_ref=source.at[part],
            dst_ref=target.at[parts - part],
            send_sem=g_send_sem.at[n, part],
            recv_sem=g_recv_sem.at[n, parts - part],
            device_id={"dp": (my_dp + part) % parts},
            device_id_type=MESH,
        )

    for part in list(range(1, parts)) + [0]:
        for n, (left, right, target) in enumerate(
            ((rows_x, d_pre, part_in), (rows_dy, scaled, part_out))
        ):

            def grads(t, carry, left=left, right=right, target=target, part=part):
                columns = pl.ds(pl.multiple_of(t * tile, tile), tile)
                target[part, columns] = contract_first(left[:, columns], right[part]).astype(BF)
                return carry

            lax.fori_loop(0, width // tile, grads, 0)
            grad_copy(n, part).start()

    d_left, d_right, g_0, g_1 = None, None, None, None
    for step in order:
        group = paired(my_group, step)
        to_x, to_dy, to_line_0, to_line_1 = selectors(group)
        await_group(back_buf, back_sem, group)
        back = back_buf[group]
        terms = (
            matmul(to_x, back),
            matmul(to_dy, back),
            matmul(to_line_0, back[:, :128]),
            matmul(to_line_1, back[:, :128]),
        )
        if d_left is None:
            d_left, d_right, g_0, g_1 = terms
        else:
            d_left, d_right, g_0, g_1 = (
                d_left + terms[0],
                d_right + terms[1],
                g_0 + terms[2],
                g_1 + terms[3],
            )
    d_tokens_ref[:, :half] = d_left.astype(BF)
    d_tokens_ref[:, half:] = d_right.astype(BF)
    first_gate = jnp.sum(jnp.where(at_slot_0, g_0, 0.0), axis=1, keepdims=True)
    second_gate = jnp.sum(jnp.where(at_slot_1, g_1, 0.0), axis=1, keepdims=True)
    gate_grad_ref[...] = jnp.where(lanes(tok_rows, 2) == 0, first_gate, second_gate).astype(BF)

    for step in range(GROUPS):
        group = paired(my_group, step)
        for turn in range(size):
            if step or turn:
                member = (my_member + turn) % size
                dispatch_copy(group, member).wait_send()
                return_copy(group, member).wait_send()
    for turn in range(1, parts):
        for n, source in enumerate((w_in_ref, w_out_ref)):
            block = source.at[0]
            pltpu.make_async_copy(block, block, w_send_sem.at[n, turn]).wait()
            grad_copy(n, turn).wait_send()
    for part in range(parts):
        for n, target in enumerate((sums_in_ref, sums_out_ref)):
            block = target.at[part]
            pltpu.make_async_copy(block, block, g_recv_sem.at[n, part]).wait()


def shards(experts, parts, tokens, out_grad, gates, expert_ids, w_in, w_out):
    tok_rows, width = tokens.shape
    hidden = w_in.shape[2]
    cap = 3 * tok_rows // experts
    chunk = -(-(2 * cap + 1) // 16) * 16
    span = experts // GROUPS * chunk
    slots = experts // GROUPS * cap
    vmem = pl.BlockSpec(memory_space=pltpu.VMEM)
    hbm = pl.BlockSpec(memory_space=pl.ANY)
    dma = pltpu.SemaphoreType.DMA
    d_tokens, gate_grad, sums_in, sums_out = pl.pallas_call(
        functools.partial(kernel, experts, parts, cap, chunk),
        out_shape=(
            jax.ShapeDtypeStruct((tok_rows, width), BF),
            jax.ShapeDtypeStruct((tok_rows, 2), BF),
            jax.ShapeDtypeStruct((parts, width, hidden), BF),
            jax.ShapeDtypeStruct((parts, width, hidden), BF),
        ),
        in_specs=[vmem, vmem, vmem, vmem, hbm, hbm],
        out_specs=(vmem, vmem, hbm, hbm),
        scratch_shapes=[
            pltpu.VMEM((GROUPS, span, width), BF),
            pltpu.VMEM((GROUPS, span, width), BF),
            pltpu.VMEM((GROUPS, span, width // 2), BF),
            pltpu.VMEM((GROUPS, span, width // 2), BF),
            pltpu.VMEM((slots, span), BF),
            pltpu.VMEM((slots, span), BF),
            pltpu.VMEM((slots, span), BF),
            pltpu.VMEM((parts, width, hidden), BF),
            pltpu.VMEM((parts, width, hidden), BF),
            pltpu.VMEM((GROUPS * slots, width), BF),
            pltpu.VMEM((GROUPS * slots, width), BF),
            pltpu.VMEM((parts, GROUPS * slots, hidden), BF),
            pltpu.VMEM((parts, GROUPS * slots, hidden), BF),
            pltpu.VMEM((parts, width, hidden), BF),
            pltpu.VMEM((parts, width, hidden), BF),
            dma((experts,)),
            dma((experts,)),
            dma((experts,)),
            dma((experts,)),
            dma((2, parts)),
            dma((2, parts)),
            dma((2, parts)),
            dma((2, parts)),
        ],
        compiler_params=pltpu.CompilerParams(
            collective_id=0, has_side_effects=True, vmem_limit_bytes=56 * 1024 * 1024
        ),
        cost_estimate=pl.CostEstimate(
            flops=10 * GROUPS * slots * width * width,
            bytes_accessed=16 * width * width,
            transcendentals=GROUPS * slots * width,
        ),
    )(tokens, out_grad, gates, expert_ids, w_in, w_out)
    return (
        d_tokens,
        gate_grad,
        jnp.sum(sums_in.astype(F32), axis=0)[None],
        jnp.sum(sums_out.astype(F32), axis=0)[None],
    )


def solution(mesh):
    split = P(("dp", "expert"), None)
    weights = P("expert", None, "dp")
    return jax.shard_map(
        functools.partial(shards, mesh.shape["expert"], mesh.shape["dp"]),
        mesh=mesh,
        in_specs=(split, split, split, split, weights, weights),
        out_specs=(split, split, weights, weights),
        check_vma=False,
    )
```

time: 201 us -> 115 us (0.57)
  Pallas kernels: 0 us -> 104 us
  waiting for transfers between devices: 83 us -> 0 us
  starting transfers between devices: 32.3 us -> 0 us
  local copies, waits for them, and re-layouts: 35.3 us -> 5.07 us
  matrix products: 22.3 us -> 0 us
  between operations: 14.1 us -> 0.64 us
  other arithmetic: 12.1 us -> 5.39 us
    pallas_call x0 -> x1, Pallas kernels: none -> 104 us  [shards(): pl.pallas_call(functools.partial(kernel, experts, parts, cap, chunk), out...]
    all_to_all x5 -> x0, waiting for transfers between devices: 81.6 us -> none  [the longest x1 28.3 us: shards(): lax.all_to_all(send_dy, 'expert', split_axis=0, concat_axis=0, tiled=True)]
    all_to_all x5 -> x0, starting transfers between devices: 32 us -> none  [the longest x1 8.31 us: shards(): lax.all_to_all(send_gate, 'expert', split_axis=0, concat_axis=0, tiled=True)]
    dot_general x6 -> x0, matrix products: 22.3 us -> none  [the longest x1 4.76 us: column_terms(): dy_proj = jnp.dot(rows_dy, w_second, preferred_element_type=jnp.float32)]
    gather x6 -> x0, local copies, waits for them, and re-layouts: 13.4 us -> none  [the longest x2 4.78 us: shards(): out_grad[source_row]]
    scatter x3 -> x0, local copies, waits for them, and re-layouts: 7.84 us -> none  [the longest x1 2.95 us: shards(): send_gate = jnp.zeros((slot_count,), jnp.bfloat16).at[target].set(gates.r...]
    reshape x8 -> x0, local copies, waits for them, and re-layouts: 6.28 us -> none  [the longest x2 2.4 us: shards(): back_dx.reshape(slot_count, model_width)[target]]
    convert_element_type x4 -> x0, other arithmetic: 5.7 us -> none  [the longest x2 5.67 us: shards(): grad_in, grad_out = (lax.psum_scatter(grad_first[None].astype(jnp.bfloat1...]
  transfers between devices with their start and end apart: 9 -> 0, of which waited for: 4 -> 0; matrix products, arithmetic and copies ran while one was open for 28% -> 0% of each run, Pallas kernels for 0% -> 0%
where the time goes in v1:
time: 115 us
  Pallas kernels  104 us (90%)
  other arithmetic  5.39 us (5%)
  local copies, waits for them, and re-layouts  5.07 us (4%)
    pallas_call x1, Pallas kernels, shards(): pl.pallas_call(functools.partial(kernel, experts, parts, cap, chunk), out...  104 us
    reduce_sum x1, other arithmetic, shards(): jnp.sum(sums_out.astype(F32), axis=0)[None]  5.39 us
    unnamed x6, local copies, waits for them, and re-layouts  5.07 us

profile of v1, /device:TPU:0, one launch (start us, length us, event | category | flops | bytes accessed | tf_op | source)
XLA Modules:
  0.0 114.7 jit_solution(4973794138886298975)
XLA Ops:
  0.6 1.4 %copy.10.gates_ref = bf16[192,2]{1,0:T(8,128)(2,1)} copy(bf16[192,2]{0,1:T(2,128)(2,1)} %param.8) | data formatting | bytes 1536 | tf_op args[2]
  2.1 1.4 %copy.11.ids_ref = s32[192,2]{1,0:T(8,128)} copy(s32[192,2]{0,1:T(2,128)} %param.9) | data formatting | bytes 3072 | tf_op args[3]
  3.5 103.6 %shard_map.93 = (bf16[192,1024]{1,0:T(8,128)(2,1)}, bf16[192,2]{1,0:T(8,128)(2,1)}, bf16[2,1024,512]{2,1,0:T(8,128)(2,1)}, bf16[2,1024,512]{2,1,0:T(8,128)(2,1)}) custom-call(bf16[192,1024]{1,0:T(8,128)(2,1)} %tokens_ref.1, bf16[192,1024]{1,0:T(8,128)(2,1)} %out_grad_ref.1, bf16[192,2]{1,0:T(8,128)(2,1)} %copy.10.gates_ref, s32[192,2]{1,0:T(8,128)} %copy.11.ids_ref, ...), custom_call_target="tpu_custom_call" | custom-call | flops 6039797760 | bytes 16777216 | tf_op jit(solution)/shard_map/pallas_call | solution.py:362
  107.1 1.5 %copy.12 = bf16[192,2]{0,1:T(2,128)(2,1)} copy(bf16[192,2]{1,0:T(8,128)(2,1)} %get-tuple-element.13) | data formatting | bytes 1536
  108.6 0.0 copy-start
  108.6 5.4 %convert_reduce_fusion = (f32[1024,512]{1,0:T(8,128)}, f32[1024,512]{1,0:T(8,128)}) fusion(bf16[2,1024,512]{2,1,0:T(8,128)(2,1)} %get-tuple-element.11, bf16[2,1024,512]{2,1,0:T(8,128)(2,1)} %get-tuple-element.10), kind=kLoop, calls=%fused_computation | loop fusion | flops 3145728 | bytes 8388608 | tf_op jit(solution)/shard_map/reduce_sum | solution.py:410
  114.0 0.0 copy-done
  114.0 0.7 copy.14
Async XLA Ops:
  108.6 5.4 %copy-start = (bf16[192,1024]{1,0:T(8,128)(2,1)S(1)}, bf16[192,1024]{1,0:T(8,128)(2,1)}, u32[]{:S(2)}) copy-start(bf16[192,1024]{1,0:T(8,128)(2,1)} %get-tuple-element.22) | copy-start | bytes 1179652

commit v2 on v1

--- a/solution.py
+++ b/solution.py
@@ -61,21 +61,23 @@
     recv_buf,
     ret_buf,
     back_buf,
-    pick_x,
-    pick_dy,
-    pick_gate,
+    ret_gate,
+    back_gate,
+    picks,
     weights_in,
     weights_out,
     rows_x,
     rows_dy,
     d_pre,
-    scaled,
+    active,
     part_in,
     part_out,
     send_sem,
     recv_sem,
     ret_sem,
     back_sem,
+    ret_gate_sem,
+    back_gate_sem,
     w_send_sem,
     w_recv_sem,
     g_send_sem,
@@ -84,9 +86,9 @@
     size = experts // GROUPS
     span = size * chunk
     slots = size * cap
+    line = 16
     tok_rows, width = tokens_ref.shape
-    half = width // 2
-    hidden = w_in_ref.shape[2]
+    half, quarter = width // 2, width // 4
     me = lax.axis_index("expert")
     my_dp = lax.axis_index("dp")
     my_group, my_member = me // size, me % size
@@ -116,8 +118,17 @@
     for copy in own_w:
         copy.start()
 
-    ids = ids_ref[...]
-    id_0, id_1 = ids[:, 0:1], ids[:, 1:2]
+    same = lax.broadcasted_iota(jnp.int32, (tok_rows, tok_rows), 0) == lanes(tok_rows, tok_rows)
+
+    def column(row):
+        return jnp.sum(jnp.where(same, row, 0.0), axis=1, keepdims=True)
+
+    def row(values):
+        return jnp.sum(jnp.where(same, values, 0.0), axis=0, keepdims=True)
+
+    ids, gates = ids_ref[...].astype(F32), gates_ref[...].astype(F32)
+    id_0, id_1 = column(ids[0:1]).astype(jnp.int32), column(ids[1:2]).astype(jnp.int32)
+    gate_0, gate_1 = column(gates[0:1]), column(gates[1:2])
     named = lanes(tok_rows, 128)
     named_0, named_1 = named == id_0, named == id_1
     later = lax.broadcasted_iota(jnp.int32, (tok_rows, tok_rows), 0) > lanes(tok_rows, tok_rows)
@@ -125,20 +136,17 @@
     slot_0 = jnp.sum(jnp.where(named_0, earlier, 0.0), axis=1, keepdims=True).astype(jnp.int32)
     slot_1 = jnp.sum(jnp.where(named_1, earlier, 0.0), axis=1, keepdims=True).astype(jnp.int32)
     place_0, place_1 = id_0 * chunk + slot_0, id_1 * chunk + slot_1
-    line_0, line_1 = id_0 * chunk + 2 * cap, id_1 * chunk + 2 * cap
-    at_slot_0, at_slot_1 = named == slot_0, named == slot_1
-    gates = gates_ref[...].astype(F32)
-    gate_0 = jnp.where(at_slot_0, gates[:, 0:1], 0.0).astype(BF)
-    gate_1 = jnp.where(at_slot_1, gates[:, 1:2], 0.0).astype(BF)
-
-    def selectors(group):
-        lane = lanes(tok_rows, span) + group * span
-        return (
-            ones_at(lane == place_0, lane == place_1),
-            ones_at(lane == place_0 + cap, lane == place_1 + cap),
-            ones_at(lane == line_0),
-            ones_at(lane == line_1),
-        )
+    line_0, line_1 = id_0 * line, id_1 * line
+
+    def selector(group, block):
+        lane = lanes(tok_rows, span) + (group * span - block * cap)
+        return ones_at(lane == place_0, lane == place_1)
+
+    def gated_selector(group, block):
+        lane = lanes(tok_rows, span) + (group * span - block * cap)
+        return jnp.where(
+            lane == place_0, gate_0, jnp.where(lane == place_1, gate_1, 0.0)
+        ).astype(BF)
 
     def chunk_rows(member):
         return pl.ds(pl.multiple_of(member * chunk, 16), chunk)
@@ -163,24 +171,35 @@
             device_id_type=MESH,
         )
 
-    def local_copy(source, target, sems):
+    def line_rows(member):
+        return pl.ds(pl.multiple_of(member * line, 16), line)
+
+    def gate_copy(group, member):
+        return pltpu.make_async_remote_copy(
+            src_ref=ret_gate.at[group, line_rows(member)],
+            dst_ref=back_gate.at[my_group, line_rows(my_member)],
+            send_sem=ret_gate_sem.at[group * size + member],
+            recv_sem=back_gate_sem.at[me],
+            device_id=expert_device(group, member),
+            device_id_type=MESH,
+        )
+
+    def local_copy(source, target, sems, rows):
         return pltpu.make_async_copy(
-            source.at[my_group, chunk_rows(my_member)],
-            target.at[my_group, chunk_rows(my_member)],
-            sems.at[me],
-        )
-
-    def await_group(target, sems, group):
+            source.at[my_group, rows], target.at[my_group, rows], sems.at[me]
+        )
+
+    def await_group(target, sems, group, rows):
         for member in range(size):
-            block = target.at[group, pl.ds(member * chunk, chunk)]
+            block = target.at[group, pl.ds(member * rows, rows)]
             pltpu.make_async_copy(block, block, sems.at[group * size + member]).wait()
 
     def fill(group):
-        to_x, to_dy, to_line_0, to_line_1 = selectors(group)
-        packed = contract_first(to_x, tokens_ref[...]) + contract_first(to_dy, out_grad_ref[...])
-        line = contract_first(to_line_0, gate_0) + contract_first(to_line_1, gate_1)
-        send_buf[group, :, 128:] = packed[:, 128:].astype(BF)
-        send_buf[group, :, :128] = (packed[:, :128] + line).astype(BF)
+        packed = contract_first(selector(group, 0), tokens_ref[:, :half])
+        packed += contract_first(selector(group, 1), tokens_ref[:, half:])
+        packed += contract_first(gated_selector(group, 2), out_grad_ref[:, :half])
+        packed += contract_first(gated_selector(group, 3), out_grad_ref[:, half:])
+        send_buf[group] = packed.astype(BF)
 
     for step in (3, 2, 1, 0):
         group = paired(my_group, step)
@@ -192,7 +211,7 @@
             if step or turn:
                 dispatch_copy(group, member).start()
             else:
-                local_copy(send_buf, recv_buf, recv_sem).start()
+                local_copy(send_buf, recv_buf, recv_sem, chunk_rows(my_member)).start()
         if step == 3:
             for turn in range(1, parts):
                 for n, (source, target) in enumerate(
@@ -208,11 +227,11 @@
                     ).start()
 
     slot = lax.broadcasted_iota(jnp.int32, (slots, 1), 0)
-    first = (slot // cap) * chunk
-    within = slot % cap
-    pick_x[...] = ones_at(lanes(slots, span) == first + within)
-    pick_dy[...] = ones_at(lanes(slots, span) == first + within + cap)
-    pick_gate[...] = ones_at(lanes(slots, span) == first + 2 * cap)
+    source = slot // cap
+    within = slot - source * cap
+    for block in range(4):
+        picks[block] = ones_at(lanes(slots, span) == source * chunk + within + block * cap)
+    to_line = ones_at(lanes(slots, size * line) == source * line)
     at_within = lanes(slots, 128) == within
 
     for copy in own_w:
@@ -227,50 +246,55 @@
     def work(turn_index, carry):
         step = turn_index + (turn_index // 2) * (5 - 2 * turn_index)
         group = paired(my_group, step)
-        await_group(recv_buf, recv_sem, group)
+        await_group(recv_buf, recv_sem, group, chunk)
         rows = pl.ds(pl.multiple_of(turn_index * slots, 16), slots)
         got = recv_buf[group]
-        x = matmul(pick_x[...], got).astype(BF)
-        dy = matmul(pick_dy[...], got).astype(BF)
-        lines = matmul(pick_gate[...], got[:, :128])
-        gate = jnp.sum(jnp.where(at_within, lines, 0.0), axis=1, keepdims=True)
-        rows_x[rows] = x
-        rows_dy[rows] = dy
+        rows_x[rows, :half] = matmul(picks[0], got).astype(BF)
+        rows_x[rows, half:] = matmul(picks[1], got).astype(BF)
+        rows_dy[rows, :half] = matmul(picks[2], got).astype(BF)
+        rows_dy[rows, half:] = matmul(picks[3], got).astype(BF)
+        x, dy = rows_x[rows], rows_dy[rows]
         dx = None
         gate_slot = None
         for part in range(parts):
             v = matmul(x, weights_in[part])
             dy_proj = matmul(dy, weights_out[part])
             tanh_inner = jnp.tanh(gelu_scale * (v + cubic_coef * v * v * v))
-            activated = (0.5 * v * (1.0 + tanh_inner)).astype(BF).astype(F32)
+            activated = (0.5 * v * (1.0 + tanh_inner)).astype(BF)
             slope = 0.5 * (1.0 + tanh_inner) + 0.5 * v * (
                 1.0 - tanh_inner * tanh_inner
             ) * gelu_scale * (1.0 + 3.0 * cubic_coef * v * v)
-            d_pre_part = (gate * dy_proj * slope).astype(BF)
+            d_pre_part = (dy_proj * slope).astype(BF)
             d_pre[part, rows] = d_pre_part
-            scaled[part, rows] = (gate * activated).astype(BF)
-            gate_part = jnp.sum(activated * dy_proj, axis=1, keepdims=True)
+            active[part, rows] = activated
+            gate_part = jnp.sum(activated.astype(F32) * dy_proj, axis=1, keepdims=True)
             dx_part = contract_last(d_pre_part, weights_in[part])
             dx = dx_part if dx is None else dx + dx_part
             gate_slot = gate_part if gate_slot is None else gate_slot + gate_part
         dx = dx.astype(BF)
-        packed = contract_first(pick_x[...], dx[:, :half]) + contract_first(
-            pick_dy[...], dx[:, half:]
-        )
-        line = contract_first(pick_gate[...], jnp.where(at_within, gate_slot, 0.0).astype(BF))
-        ret_buf[group, :, 128:] = packed[:, 128:].astype(BF)
-        ret_buf[group, :, :128] = (packed[:, :128] + line).astype(BF)
+        packed = contract_first(picks[0], dx[:, :quarter])
+        for block in range(1, 4):
+            packed += contract_first(
+                picks[block], dx[:, block * quarter : (block + 1) * quarter]
+            )
+        ret_buf[group] = packed.astype(BF)
+        ret_gate[group] = contract_first(
+            to_line, jnp.where(at_within, gate_slot, 0.0).astype(BF)
+        ).astype(BF)
 
         for turn in range(1, size):
             return_copy(group, (my_member + turn) % size).start()
+            gate_copy(group, (my_member + turn) % size).start()
 
         @pl.when(turn_index == 0)
         def _():
-            local_copy(ret_buf, back_buf, back_sem).start()
+            local_copy(ret_buf, back_buf, back_sem, chunk_rows(my_member)).start()
+            local_copy(ret_gate, back_gate, back_gate_sem, line_rows(my_member)).start()
 
         @pl.when(turn_index > 0)
         def _():
             return_copy(group, my_member).start()
+            gate_copy(group, my_member).start()
 
         return carry
 
@@ -293,7 +317,7 @@
 
     for part in list(range(1, parts)) + [0]:
         for n, (left, right, target) in enumerate(
-            ((rows_x, d_pre, part_in), (rows_dy, scaled, part_out))
+            ((rows_x, d_pre, part_in), (rows_dy, active, part_out))
         ):
 
             def grads(t, carry, left=left, right=right, target=target, part=part):
@@ -304,32 +328,24 @@
             lax.fori_loop(0, width // tile, grads, 0)
             grad_copy(n, part).start()
 
-    d_left, d_right, g_0, g_1 = None, None, None, None
+    totals = None
     for step in order:
         group = paired(my_group, step)
-        to_x, to_dy, to_line_0, to_line_1 = selectors(group)
-        await_group(back_buf, back_sem, group)
-        back = back_buf[group]
-        terms = (
-            matmul(to_x, back),
-            matmul(to_dy, back),
-            matmul(to_line_0, back[:, :128]),
-            matmul(to_line_1, back[:, :128]),
-        )
-        if d_left is None:
-            d_left, d_right, g_0, g_1 = terms
-        else:
-            d_left, d_right, g_0, g_1 = (
-                d_left + terms[0],
-                d_right + terms[1],
-                g_0 + terms[2],
-                g_1 + terms[3],
-            )
-    d_tokens_ref[:, :half] = d_left.astype(BF)
-    d_tokens_ref[:, half:] = d_right.astype(BF)
-    first_gate = jnp.sum(jnp.where(at_slot_0, g_0, 0.0), axis=1, keepdims=True)
-    second_gate = jnp.sum(jnp.where(at_slot_1, g_1, 0.0), axis=1, keepdims=True)
-    gate_grad_ref[...] = jnp.where(lanes(tok_rows, 2) == 0, first_gate, second_gate).astype(BF)
+        selectors = [selector(group, block) for block in range(4)]
+        lane = lanes(tok_rows, size * line) + group * size * line
+        from_lines = ones_at(lane == line_0), ones_at(lane == line_1)
+        await_group(back_gate, back_gate_sem, group, line)
+        await_group(back_buf, back_sem, group, chunk)
+        back, lines = back_buf[group], back_gate[group]
+        terms = [matmul(chosen, back) for chosen in selectors]
+        terms += [matmul(chosen, lines) for chosen in from_lines]
+        totals = terms if totals is None else [a + b for a, b in zip(totals, terms)]
+    for block in range(4):
+        d_tokens_ref[:, block * quarter : (block + 1) * quarter] = totals[block].astype(BF)
+    first_gate = jnp.sum(jnp.where(named == slot_0, totals[4], 0.0), axis=1, keepdims=True)
+    second_gate = jnp.sum(jnp.where(named == slot_1, totals[5], 0.0), axis=1, keepdims=True)
+    gate_grad_ref[0:1] = row(first_gate / gate_0).astype(BF)
+    gate_grad_ref[1:2] = row(second_gate / gate_1).astype(BF)
 
     for step in range(GROUPS):
         group = paired(my_group, step)
@@ -338,6 +354,7 @@
                 member = (my_member + turn) % size
                 dispatch_copy(group, member).wait_send()
                 return_copy(group, member).wait_send()
+                gate_copy(group, member).wait_send()
     for turn in range(1, parts):
         for n, source in enumerate((w_in_ref, w_out_ref)):
             block = source.at[0]
@@ -353,30 +370,31 @@
     tok_rows, width = tokens.shape
     hidden = w_in.shape[2]
     cap = 3 * tok_rows // experts
-    chunk = -(-(2 * cap + 1) // 16) * 16
+    chunk = -(-4 * cap // 16) * 16
     span = experts // GROUPS * chunk
     slots = experts // GROUPS * cap
     vmem = pl.BlockSpec(memory_space=pltpu.VMEM)
-    hbm = pl.BlockSpec(memory_space=pl.ANY)
+    hbm = pl.BlockSpec(memory_space=pltpu.HBM)
+    free = pl.BlockSpec(memory_space=pl.ANY)
     dma = pltpu.SemaphoreType.DMA
     d_tokens, gate_grad, sums_in, sums_out = pl.pallas_call(
         functools.partial(kernel, experts, parts, cap, chunk),
         out_shape=(
             jax.ShapeDtypeStruct((tok_rows, width), BF),
-            jax.ShapeDtypeStruct((tok_rows, 2), BF),
+            jax.ShapeDtypeStruct((2, tok_rows), BF),
             jax.ShapeDtypeStruct((parts, width, hidden), BF),
             jax.ShapeDtypeStruct((parts, width, hidden), BF),
         ),
         in_specs=[vmem, vmem, vmem, vmem, hbm, hbm],
-        out_specs=(vmem, vmem, hbm, hbm),
+        out_specs=(vmem, vmem, free, free),
         scratch_shapes=[
-            pltpu.VMEM((GROUPS, span, width), BF),
-            pltpu.VMEM((GROUPS, span, width), BF),
             pltpu.VMEM((GROUPS, span, width // 2), BF),
             pltpu.VMEM((GROUPS, span, width // 2), BF),
-            pltpu.VMEM((slots, span), BF),
-            pltpu.VMEM((slots, span), BF),
-            pltpu.VMEM((slots, span), BF),
+            pltpu.VMEM((GROUPS, span, width // 4), BF),
+            pltpu.VMEM((GROUPS, span, width // 4), BF),
+            pltpu.VMEM((GROUPS, experts // GROUPS * 16, 128), BF),
+            pltpu.VMEM((GROUPS, experts // GROUPS * 16, 128), BF),
+            pltpu.VMEM((4, slots, span), BF),
             pltpu.VMEM((parts, width, hidden), BF),
             pltpu.VMEM((parts, width, hidden), BF),
             pltpu.VMEM((GROUPS * slots, width), BF),
@@ -389,23 +407,25 @@
             dma((experts,)),
             dma((experts,)),
             dma((experts,)),
+            dma((experts,)),
+            dma((experts,)),
             dma((2, parts)),
             dma((2, parts)),
             dma((2, parts)),
             dma((2, parts)),
         ],
         compiler_params=pltpu.CompilerParams(
-            collective_id=0, has_side_effects=True, vmem_limit_bytes=56 * 1024 * 1024
+            collective_id=0, has_side_effects=True, vmem_limit_bytes=36 * 1024 * 1024
         ),
         cost_estimate=pl.CostEstimate(
             flops=10 * GROUPS * slots * width * width,
             bytes_accessed=16 * width * width,
             transcendentals=GROUPS * slots * width,
         ),
-    )(tokens, out_grad, gates, expert_ids, w_in, w_out)
+    )(tokens, out_grad, gates.T, expert_ids.T, w_in, w_out)
     return (
         d_tokens,
-        gate_grad,
+        gate_grad.T,
         jnp.sum(sums_in.astype(F32), axis=0)[None],
         jnp.sum(sums_out.astype(F32), axis=0)[None],
     )

time: 115 us -> 104 us (0.904)
  Pallas kernels: 104 us -> 93.4 us
  other arithmetic: 5.39 us -> 2.77 us
  local copies, waits for them, and re-layouts: 5.07 us -> 7.1 us
    pallas_call x1, Pallas kernels: 104 us -> 93.4 us  [shards(): pl.pallas_call(functools.partial(kernel, experts, parts, cap, chunk), out...]
    reduce_sum x1, other arithmetic: 5.39 us -> 2.77 us  [shards(): jnp.sum(sums_out.astype(F32), axis=0)[None]]
    unnamed x6 -> x14, local copies, waits for them, and re-layouts: 5.07 us -> 7.1 us
where the time goes in v2:
time: 104 us
  Pallas kernels  93.4 us (90%)
  local copies, waits for them, and re-layouts  7.1 us (7%)
  other arithmetic  2.77 us (3%)
    pallas_call x1, Pallas kernels, shards(): pl.pallas_call(functools.partial(kernel, experts, parts, cap, chunk), out...  93.4 us
    unnamed x14, local copies, waits for them, and re-layouts  7.1 us
    reduce_sum x1, other arithmetic, shards(): jnp.sum(sums_out.astype(F32), axis=0)[None]  2.77 us

profile of v2, /device:TPU:0, one launch (start us, length us, event | category | flops | bytes accessed | tf_op | source)
XLA Modules:
  0.0 103.9 jit_solution(13975646205053037616)
XLA Ops:
  0.6 0.0 copy-start
  0.6 1.2 %copy-done = bf16[1,1024,512]{2,1,0:T(8,128)(2,1)S(1)} copy-done((bf16[1,1024,512]{2,1,0:T(8,128)(2,1)S(1)}, bf16[1,1024,512]{2,1,0:T(8,128)(2,1)}, u32[]{:S(2)}) %copy-start) | copy-done | bytes 1048600
  1.9 0.0 copy-start.1
  1.9 1.2 %copy-done.1 = bf16[1,1024,512]{2,1,0:T(8,128)(2,1)S(1)} copy-done((bf16[1,1024,512]{2,1,0:T(8,128)(2,1)S(1)}, bf16[1,1024,512]{2,1,0:T(8,128)(2,1)}, u32[]{:S(2)}) %copy-start.1) | copy-done | bytes 1048600
  3.1 0.0 copy-start.2
  3.1 1.0 copy-done.2
  4.1 0.0 copy-start.3
  4.1 1.0 copy-done.3
  5.1 0.0 copy-start.4
  5.1 0.7 copy-done.4
  5.8 0.0 copy-start.5
  5.8 0.7 copy-done.5
  6.4 93.4 %shard_map.93 = (bf16[192,1024]{1,0:T(8,128)(2,1)S(1)}, bf16[2,192]{1,0:T(2,128)(2,1)S(1)}, bf16[2,1024,512]{2,1,0:T(8,128)(2,1)S(1)}, bf16[2,1024,512]{2,1,0:T(8,128)(2,1)S(1)}) custom-call(bf16[192,1024]{1,0:T(8,128)(2,1)S(1)} %copy-done.2, bf16[192,1024]{1,0:T(8,128)(2,1)S(1)} %copy-done.3, bf16[2,192]{1,0:T(2,128)(2,1)S(1)} %bitcast.7, ...), custom_call_target="tpu_custom_call" | custom-call | flops 6039797760 | bytes 16777216 | tf_op jit(solution)/shard_map/pallas_call | solution.py:380
  99.8 2.8 %convert_reduce_fusion = (f32[1024,512]{1,0:T(8,128)}, f32[1024,512]{1,0:T(8,128)}) fusion(bf16[2,1024,512]{2,1,0:T(8,128)(2,1)S(1)} %get-tuple-element.11, bf16[2,1024,512]{2,1,0:T(8,128)(2,1)S(1)} %get-tuple-element.10), kind=kLoop, calls=%fused_computation | loop fusion | flops 3145728 | bytes 8388608 | tf_op jit(solution)/shard_map/reduce_sum | solution.py:430
  102.6 0.7 copy.12
  103.4 0.6 copy.13
Async XLA Ops:
  0.6 1.2 %copy-start = (bf16[1,1024,512]{2,1,0:T(8,128)(2,1)S(1)}, bf16[1,1024,512]{2,1,0:T(8,128)(2,1)}, u32[]{:S(2)}) copy-start(bf16[1,1024,512]{2,1,0:T(8,128)(2,1)} %w_in_ref.1) | copy-start | bytes 3145732
  1.9 1.2 %copy-start.1 = (bf16[1,1024,512]{2,1,0:T(8,128)(2,1)S(1)}, bf16[1,1024,512]{2,1,0:T(8,128)(2,1)}, u32[]{:S(2)}) copy-start(bf16[1,1024,512]{2,1,0:T(8,128)(2,1)} %w_out_ref.1) | copy-start | bytes 3145732
  3.1 1.0 copy-start.2
  4.1 1.0 copy-start.3
  5.1 0.7 copy-start.4
  5.8 0.7 copy-start.5

commit v3 on v2

--- a/solution.py
+++ b/solution.py
@@ -47,8 +47,8 @@
     parts,
     cap,
     chunk,
-    tokens_ref,
-    out_grad_ref,
+    tokens_hbm,
+    out_grad_hbm,
     gates_ref,
     ids_ref,
     w_in_ref,
@@ -57,6 +57,8 @@
     gate_grad_ref,
     sums_in_ref,
     sums_out_ref,
+    tokens_ref,
+    out_grad_ref,
     send_buf,
     recv_buf,
     ret_buf,
@@ -82,6 +84,7 @@
     w_recv_sem,
     g_send_sem,
     g_recv_sem,
+    token_sem,
 ):
     size = experts // GROUPS
     span = size * chunk
@@ -95,6 +98,13 @@
 
     def expert_device(group, member):
         return {"expert": group * size + member}
+
+    own_rows = [
+        pltpu.make_async_copy(tokens_hbm, tokens_ref, token_sem.at[0]),
+        pltpu.make_async_copy(out_grad_hbm, out_grad_ref, token_sem.at[1]),
+    ]
+    for copy in own_rows:
+        copy.start()
 
     barrier = pltpu.get_barrier_semaphore()
     for step in range(GROUPS):
@@ -142,8 +152,12 @@
         lane = lanes(tok_rows, span) + (group * span - block * cap)
         return ones_at(lane == place_0, lane == place_1)
 
-    def gated_selector(group, block):
-        lane = lanes(tok_rows, span) + (group * span - block * cap)
+    def chunk_selector(start, block):
+        lane = lanes(tok_rows, chunk) + (start - block * cap)
+        return ones_at(lane == place_0, lane == place_1)
+
+    def gated_selector(start, block):
+        lane = lanes(tok_rows, chunk) + (start - block * cap)
         return jnp.where(
             lane == place_0, gate_0, jnp.where(lane == place_1, gate_1, 0.0)
         ).astype(BF)
@@ -194,37 +208,43 @@
             block = target.at[group, pl.ds(member * rows, rows)]
             pltpu.make_async_copy(block, block, sems.at[group * size + member]).wait()
 
-    def fill(group):
-        packed = contract_first(selector(group, 0), tokens_ref[:, :half])
-        packed += contract_first(selector(group, 1), tokens_ref[:, half:])
-        packed += contract_first(gated_selector(group, 2), out_grad_ref[:, :half])
-        packed += contract_first(gated_selector(group, 3), out_grad_ref[:, half:])
-        send_buf[group] = packed.astype(BF)
-
-    for step in (3, 2, 1, 0):
-        group = paired(my_group, step)
-        fill(group)
-        if step == 3:
-            pl.semaphore_wait(barrier, experts - 1 + parts - 1)
-        for turn in range(size):
-            member = (my_member + turn) % size
-            if step or turn:
-                dispatch_copy(group, member).start()
-            else:
-                local_copy(send_buf, recv_buf, recv_sem, chunk_rows(my_member)).start()
-        if step == 3:
-            for turn in range(1, parts):
-                for n, (source, target) in enumerate(
-                    ((w_in_ref, weights_in), (w_out_ref, weights_out))
-                ):
-                    pltpu.make_async_remote_copy(
-                        src_ref=source.at[0],
-                        dst_ref=target.at[parts - turn],
-                        send_sem=w_send_sem.at[n, turn],
-                        recv_sem=w_recv_sem.at[n, parts - turn],
-                        device_id={"dp": (my_dp + turn) % parts},
-                        device_id_type=MESH,
-                    ).start()
+    def fill(group, member):
+        start = (group * size + member) * chunk
+        packed = contract_first(chunk_selector(start, 0), tokens_ref[:, :half])
+        packed += contract_first(chunk_selector(start, 1), tokens_ref[:, half:])
+        packed += contract_first(gated_selector(start, 2), out_grad_ref[:, :half])
+        packed += contract_first(gated_selector(start, 3), out_grad_ref[:, half:])
+        send_buf[group, chunk_rows(member)] = packed.astype(BF)
+
+    def fill_and_send(step, turn):
+        group, member = paired(my_group, step), (my_member + turn) % size
+        fill(group, member)
+        dispatch_copy(group, member).start()
+
+    for copy in own_rows:
+        copy.wait()
+    fill(paired(my_group, 3), my_member)
+    pl.semaphore_wait(barrier, experts - 1 + parts - 1)
+    dispatch_copy(paired(my_group, 3), my_member).start()
+    for turn in range(1, parts):
+        for n, (source, target) in enumerate(((w_in_ref, weights_in), (w_out_ref, weights_out))):
+            pltpu.make_async_remote_copy(
+                src_ref=source.at[0],
+                dst_ref=target.at[parts - turn],
+                send_sem=w_send_sem.at[n, turn],
+                recv_sem=w_recv_sem.at[n, parts - turn],
+                device_id={"dp": (my_dp + turn) % parts},
+                device_id_type=MESH,
+            ).start()
+
+    def others(count, carry):
+        fill_and_send(3 - count // size, count % size)
+        return carry
+
+    lax.fori_loop(1, 3 * size, others, 0)
+    fill(my_group, my_member)
+    local_copy(send_buf, recv_buf, recv_sem, chunk_rows(my_member)).start()
+    lax.fori_loop(3 * size + 1, 4 * size, others, 0)
 
     slot = lax.broadcasted_iota(jnp.int32, (slots, 1), 0)
     source = slot // cap
@@ -366,6 +386,10 @@
             pltpu.make_async_copy(block, block, g_recv_sem.at[n, part]).wait()
 
 
+def stay(array):
+    return pltpu.with_memory_space_constraint(array, pltpu.HBM)
+
+
 def shards(experts, parts, tokens, out_grad, gates, expert_ids, w_in, w_out):
     tok_rows, width = tokens.shape
     hidden = w_in.shape[2]
@@ -385,9 +409,11 @@
             jax.ShapeDtypeStruct((parts, width, hidden), BF),
             jax.ShapeDtypeStruct((parts, width, hidden), BF),
         ),
-        in_specs=[vmem, vmem, vmem, vmem, hbm, hbm],
+        in_specs=[hbm, hbm, vmem, vmem, hbm, hbm],
         out_specs=(vmem, vmem, free, free),
         scratch_shapes=[
+            pltpu.VMEM((tok_rows, width), BF),
+            pltpu.VMEM((tok_rows, width), BF),
             pltpu.VMEM((GROUPS, span, width // 2), BF),
             pltpu.VMEM((GROUPS, span, width // 2), BF),
             pltpu.VMEM((GROUPS, span, width // 4), BF),
@@ -413,6 +439,7 @@
             dma((2, parts)),
             dma((2, parts)),
             dma((2, parts)),
+            dma((2,)),
         ],
         compiler_params=pltpu.CompilerParams(
             collective_id=0, has_side_effects=True, vmem_limit_bytes=36 * 1024 * 1024
@@ -422,7 +449,9 @@
             bytes_accessed=16 * width * width,
             transcendentals=GROUPS * slots * width,
         ),
-    )(tokens, out_grad, gates.T, expert_ids.T, w_in, w_out)
+    )(
+        *map(stay, (tokens, out_grad, gates.T, expert_ids.T, w_in, w_out))
+    )
     return (
         d_tokens,
         gate_grad.T,

time: 104 us -> 98.5 us (0.947)
  local copies, waits for them, and re-layouts: 7.1 us -> 1.31 us
    unnamed x14 -> x2, local copies, waits for them, and re-layouts: 7.1 us -> 1.31 us
where the time goes in v3:
time: 98.5 us; the launch traced here: 98.3 us
  Pallas kernels  93.6 us (95%)
  other arithmetic  2.78 us (3%)
  local copies, waits for them, and re-layouts  1.31 us (1%)
    pallas_call x1, Pallas kernels, shards(): pl.pallas_call(functools.partial(kernel, experts, parts, cap, chunk), out...  93.6 us
    reduce_sum x1, other arithmetic, shards(): jnp.sum(sums_out.astype(F32), axis=0)[None]  2.78 us

profile of v3, /device:TPU:0, one launch (start us, length us, event | category | flops | bytes accessed | tf_op | source)
XLA Modules:
  0.0 98.3 jit_solution(1580378723503981526)
XLA Ops:
  0.6 93.6 %shard_map.93 = (bf16[192,1024]{1,0:T(8,128)(2,1)S(1)}, bf16[2,192]{1,0:T(2,128)(2,1)S(1)}, bf16[2,1024,512]{2,1,0:T(8,128)(2,1)S(1)}, bf16[2,1024,512]{2,1,0:T(8,128)(2,1)S(1)}) custom-call(bf16[192,1024]{1,0:T(8,128)(2,1)} %tokens_hbm.1, bf16[192,1024]{1,0:T(8,128)(2,1)} %out_grad_hbm.1, bf16[2,192]{1,0:T(2,128)(2,1)} %bitcast.9, s32[2,192]{1,0:T(2,128)} %bitcast.8, ...), custom_call_target="tpu_custom_call" | custom-call | flops 6039797760 | bytes 16777216 | tf_op jit(solution)/shard_map/pallas_call | solution.py:404
  94.2 2.8 %convert_reduce_fusion = (f32[1024,512]{1,0:T(8,128)}, f32[1024,512]{1,0:T(8,128)}) fusion(bf16[2,1024,512]{2,1,0:T(8,128)(2,1)S(1)} %get-tuple-element.11, bf16[2,1024,512]{2,1,0:T(8,128)(2,1)S(1)} %get-tuple-element.10), kind=kLoop, calls=%fused_computation | loop fusion | flops 3145728 | bytes 8388608 | tf_op jit(solution)/shard_map/reduce_sum | solution.py:459
  97.0 0.7 copy.12
  97.8 0.6 copy.13

commit v4 on v3

--- a/solution.py
+++ b/solution.py
@@ -57,8 +57,7 @@
     gate_grad_ref,
     sums_in_ref,
     sums_out_ref,
-    tokens_ref,
-    out_grad_ref,
+    quarters,
     send_buf,
     recv_buf,
     ret_buf,
@@ -90,7 +89,7 @@
     span = size * chunk
     slots = size * cap
     line = 16
-    tok_rows, width = tokens_ref.shape
+    tok_rows, width = tokens_hbm.shape
     half, quarter = width // 2, width // 4
     me = lax.axis_index("expert")
     my_dp = lax.axis_index("dp")
@@ -100,8 +99,13 @@
         return {"expert": group * size + member}
 
     own_rows = [
-        pltpu.make_async_copy(tokens_hbm, tokens_ref, token_sem.at[0]),
-        pltpu.make_async_copy(out_grad_hbm, out_grad_ref, token_sem.at[1]),
+        pltpu.make_async_copy(
+            whole.at[:, pl.ds(side * half, half)],
+            quarters.at[pl.ds((2 * n + side) * tok_rows, tok_rows)],
+            token_sem.at[2 * n + side],
+        )
+        for n, whole in enumerate((tokens_hbm, out_grad_hbm))
+        for side in range(2)
     ]
     for copy in own_rows:
         copy.start()
@@ -210,10 +214,9 @@
 
     def fill(group, member):
         start = (group * size + member) * chunk
-        packed = contract_first(chunk_selector(start, 0), tokens_ref[:, :half])
-        packed += contract_first(chunk_selector(start, 1), tokens_ref[:, half:])
-        packed += contract_first(gated_selector(start, 2), out_grad_ref[:, :half])
-        packed += contract_first(gated_selector(start, 3), out_grad_ref[:, half:])
+        chosen = [chunk_selector(start, block) for block in (0, 1)]
+        chosen += [gated_selector(start, block) for block in (2, 3)]
+        packed = contract_first(jnp.concatenate(chosen, axis=0), quarters[...])
         send_buf[group, chunk_rows(member)] = packed.astype(BF)
 
     def fill_and_send(step, turn):
@@ -250,7 +253,9 @@
     source = slot // cap
     within = slot - source * cap
     for block in range(4):
-        picks[block] = ones_at(lanes(slots, span) == source * chunk + within + block * cap)
+        picks[block * slots : (block + 1) * slots] = ones_at(
+            lanes(slots, span) == source * chunk + within + block * cap
+        )
     to_line = ones_at(lanes(slots, size * line) == source * line)
     at_within = lanes(slots, 128) == within
 
@@ -269,10 +274,11 @@
         await_group(recv_buf, recv_sem, group, chunk)
         rows = pl.ds(pl.multiple_of(turn_index * slots, 16), slots)
         got = recv_buf[group]
-        rows_x[rows, :half] = matmul(picks[0], got).astype(BF)
-        rows_x[rows, half:] = matmul(picks[1], got).astype(BF)
-        rows_dy[rows, :half] = matmul(picks[2], got).astype(BF)
-        rows_dy[rows, half:] = matmul(picks[3], got).astype(BF)
+        got = matmul(picks[...], got).astype(BF)
+        rows_x[rows, :half] = got[:slots]
+        rows_x[rows, half:] = got[slots : 2 * slots]
+        rows_dy[rows, :half] = got[2 * slots : 3 * slots]
+        rows_dy[rows, half:] = got[3 * slots :]
         x, dy = rows_x[rows], rows_dy[rows]
         dx = None
         gate_slot = None
@@ -292,11 +298,8 @@
             dx = dx_part if dx is None else dx + dx_part
             gate_slot = gate_part if gate_slot is None else gate_slot + gate_part
         dx = dx.astype(BF)
-        packed = contract_first(picks[0], dx[:, :quarter])
-        for block in range(1, 4):
-            packed += contract_first(
-                picks[block], dx[:, block * quarter : (block + 1) * quarter]
-            )
+        stacked = [dx[:, block * quarter : (block + 1) * quarter] for block in range(4)]
+        packed = contract_first(picks[...], jnp.concatenate(stacked, axis=0))
         ret_buf[group] = packed.astype(BF)
         ret_gate[group] = contract_first(
             to_line, jnp.where(at_within, gate_slot, 0.0).astype(BF)
@@ -351,19 +354,19 @@
     totals = None
     for step in order:
         group = paired(my_group, step)
-        selectors = [selector(group, block) for block in range(4)]
+        chosen = jnp.concatenate([selector(group, block) for block in range(4)], axis=0)
         lane = lanes(tok_rows, size * line) + group * size * line
-        from_lines = ones_at(lane == line_0), ones_at(lane == line_1)
+        from_lines = jnp.concatenate((ones_at(lane == line_0), ones_at(lane == line_1)), axis=0)
         await_group(back_gate, back_gate_sem, group, line)
         await_group(back_buf, back_sem, group, chunk)
-        back, lines = back_buf[group], back_gate[group]
-        terms = [matmul(chosen, back) for chosen in selectors]
-        terms += [matmul(chosen, lines) for chosen in from_lines]
+        terms = [matmul(chosen, back_buf[group]), matmul(from_lines, back_gate[group])]
         totals = terms if totals is None else [a + b for a, b in zip(totals, terms)]
     for block in range(4):
-        d_tokens_ref[:, block * quarter : (block + 1) * quarter] = totals[block].astype(BF)
-    first_gate = jnp.sum(jnp.where(named == slot_0, totals[4], 0.0), axis=1, keepdims=True)
-    second_gate = jnp.sum(jnp.where(named == slot_1, totals[5], 0.0), axis=1, keepdims=True)
+        d_tokens_ref[:, block * quarter : (block + 1) * quarter] = totals[0][
+            block * tok_rows : (block + 1) * tok_rows
+        ].astype(BF)
+    first_gate = jnp.sum(jnp.where(named == slot_0, totals[1][:tok_rows], 0.0), axis=1, keepdims=True)
+    second_gate = jnp.sum(jnp.where(named == slot_1, totals[1][tok_rows:], 0.0), axis=1, keepdims=True)
     gate_grad_ref[0:1] = row(first_gate / gate_0).astype(BF)
     gate_grad_ref[1:2] = row(second_gate / gate_1).astype(BF)
 
@@ -412,15 +415,14 @@
         in_specs=[hbm, hbm, vmem, vmem, hbm, hbm],
         out_specs=(vmem, vmem, free, free),
         scratch_shapes=[
-            pltpu.VMEM((tok_rows, width), BF),
-            pltpu.VMEM((tok_rows, width), BF),
+            pltpu.VMEM((4 * tok_rows, width // 2), BF),
             pltpu.VMEM((GROUPS, span, width // 2), BF),
             pltpu.VMEM((GROUPS, span, width // 2), BF),
             pltpu.VMEM((GROUPS, span, width // 4), BF),
             pltpu.VMEM((GROUPS, span, width // 4), BF),
             pltpu.VMEM((GROUPS, experts // GROUPS * 16, 128), BF),
             pltpu.VMEM((GROUPS, experts // GROUPS * 16, 128), BF),
-            pltpu.VMEM((4, slots, span), BF),
+            pltpu.VMEM((4 * slots, span), BF),
             pltpu.VMEM((parts, width, hidden), BF),
             pltpu.VMEM((parts, width, hidden), BF),
             pltpu.VMEM((GROUPS * slots, width), BF),
@@ -439,7 +441,7 @@
             dma((2, parts)),
             dma((2, parts)),
             dma((2, parts)),
-            dma((2,)),
+            dma((4,)),
         ],
         compiler_params=pltpu.CompilerParams(
             collective_id=0, has_side_effects=True, vmem_limit_bytes=36 * 1024 * 1024

time: 98.5 us -> 98.6 us (level)
  no operation moved by 1% of the time
where the time goes in v4:
time: 98.6 us; the launch traced here: 98.4 us
  Pallas kernels  93.7 us (95%)
  other arithmetic  2.78 us (3%)
  local copies, waits for them, and re-layouts  1.31 us (1%)
    pallas_call x1, Pallas kernels, shards(): pl.pallas_call(functools.partial(kernel, experts, parts, cap, chunk), out...  93.7 us
    reduce_sum x1, other arithmetic, shards(): jnp.sum(sums_out.astype(F32), axis=0)[None]  2.78 us

profile of v4, /device:TPU:0, one launch (start us, length us, event | category | flops | bytes accessed | tf_op | source)
XLA Modules:
  0.0 98.4 jit_solution(15309415285072478870)
XLA Ops:
  0.6 93.7 %shard_map.93 = (bf16[192,1024]{1,0:T(8,128)(2,1)S(1)}, bf16[2,192]{1,0:T(2,128)(2,1)S(1)}, bf16[2,1024,512]{2,1,0:T(8,128)(2,1)S(1)}, bf16[2,1024,512]{2,1,0:T(8,128)(2,1)S(1)}) custom-call(bf16[192,1024]{1,0:T(8,128)(2,1)} %tokens_hbm.1, bf16[192,1024]{1,0:T(8,128)(2,1)} %out_grad_hbm.1, bf16[2,192]{1,0:T(2,128)(2,1)} %bitcast.9, s32[2,192]{1,0:T(2,128)} %bitcast.8, ...), custom_call_target="tpu_custom_call" | custom-call | flops 6039797760 | bytes 16777216 | tf_op jit(solution)/shard_map/pallas_call | solution.py:407
  94.4 2.8 %convert_reduce_fusion = (f32[1024,512]{1,0:T(8,128)}, f32[1024,512]{1,0:T(8,128)}) fusion(bf16[2,1024,512]{2,1,0:T(8,128)(2,1)S(1)} %get-tuple-element.11, bf16[2,1024,512]{2,1,0:T(8,128)(2,1)S(1)} %get-tuple-element.10), kind=kLoop, calls=%fused_computation | loop fusion | flops 3145728 | bytes 8388608 | tf_op jit(solution)/shard_map/reduce_sum | solution.py:461
  97.1 0.7 copy.12
  97.9 0.6 copy.13
